TPU v7x, 32 devices: a whole 2x2x4 slice. The times are simulated.
32 devices in a mesh: var: 8 (over y, x, core), seq: 4 (over z).
Axes of the slice: x: 2, y: 2, z: 4, core: 2. Of those that a mesh axis runs over, the one named last changes fastest.
Arguments:
- patches: bfloat16 [48, 512, 64], P('var', 'seq'), may hold values from -6 to 6
- patch_weight: bfloat16 [48, 64, 4096], P('var'), may hold values from -0.75 to 0.75
- var_embed: bfloat16 [48, 4096], P('var'), may hold values from -1.71 to 4.5
- agg_query: bfloat16 [4096, 32], replicated, may hold values from -1.5 to 1000
- norm_gain: bfloat16 [4096], replicated, may hold values from 0.5 to 1.5
- qkv_weight: bfloat16 [4096, 3, 4096], P(None, None, 'var'), may hold values from -0.21875 to 0.21875
- out_weight: bfloat16 [4096, 4096], P('var'), may hold values from -0.09375 to 0.09375
- head_cot: bfloat16 [512, 3072], P('seq', 'var'), may hold values from -0.25 to 0.25
Outputs:
- head_grad: float32 [4096, 3072], P('seq', 'var')
All inputs are finite; a program needn't handle non-finite values.
Results may differ from a plain program's by a relative error of at most 0.033.
The roundings to bfloat16 on the way count: a program that leaves them out, or rounds other values in their place, can miss the bound.
Values may be sent and summed in bfloat16 or wider, within the bound.
A program may use at most 128 MiB of HBM per device.

v0:
```python
import math

import jax
import jax.numpy as jnp
from jax import lax
from jax.sharding import PartitionSpec as P

eps = 1e-05


def merged(array, axis, combine):
    everything = jax.tree.map(lambda part: lax.all_gather(part, axis), array)
    initial = jax.tree.map(lambda part: part[0], everything)

    def turn(k, so_far):
        return combine(so_far, jax.tree.map(lambda part: part[k], everything))

    return lax.fori_loop(1, lax.axis_size(axis), turn, initial)


def layer_norm(tokens, gain):
    values = tokens.astype(jnp.float32)
    center = jnp.mean(values, axis=-1, keepdims=True)
    shifted = values - center
    spread = jnp.mean(shifted * shifted, axis=-1, keepdims=True)
    return (shifted * lax.rsqrt(spread + eps) * gain.astype(jnp.float32)).astype(jnp.bfloat16)


def combine_parts(first_part, second_part):
    top_a, total_a, numer_a = first_part
    top_b, total_b, numer_b = second_part
    top = jnp.maximum(top_a, top_b)
    scale_a = jnp.exp(top_a - top)
    scale_b = jnp.exp(top_b - top)
    total = total_a * scale_a + total_b * scale_b
    numer = numer_a * scale_a[..., None] + numer_b * scale_b[..., None]
    return (top, total, numer)


def body(patches, patch_weight, var_embed, agg_query, norm_gain, qkv_weight, out_weight, head_cot):
    count, tok_rows, pixels = patches.shape
    width = patch_weight.shape[2]
    heads = agg_query.shape[1]
    head_size = width // heads
    share = tok_rows // lax.axis_size("var")
    first_row = lax.axis_index("var") * share
    embedded = jnp.einsum("vrp,vpd->vrd", patches, patch_weight, preferred_element_type=jnp.float32)
    embedded = (embedded + var_embed.astype(jnp.float32)[:, None, :]).astype(jnp.bfloat16)
    scores = jnp.dot(
        embedded.reshape(count * tok_rows, width), agg_query, preferred_element_type=jnp.float32
    )
    scores = scores.reshape(count, tok_rows, heads) / math.sqrt(head_size)
    peak = jnp.max(scores, axis=0)
    weights = jnp.exp(scores - peak[None])
    total = jnp.sum(weights, axis=0)
    numer = jnp.zeros((tok_rows, heads, head_size), jnp.float32)
    for member in range(count):
        numer = numer + weights[member][..., None] * embedded[member].reshape(
            tok_rows, heads, head_size
        ).astype(jnp.float32)
    total, numer = (total, numer)
    top, total, numer = merged((peak, total, numer), "var", combine_parts)
    whole = (numer / total[..., None]).reshape(tok_rows, width).astype(jnp.bfloat16)
    own_rows = lax.dynamic_slice_in_dim(whole, first_row, share, 0)
    normed = layer_norm(whole, norm_gain)
    local_cols = qkv_weight.shape[2]
    local_heads = local_cols // head_size
    qkv = jnp.dot(
        normed, qkv_weight.reshape(width, 3 * local_cols), preferred_element_type=jnp.float32
    )
    qkv = qkv.astype(jnp.bfloat16).reshape(tok_rows, 3, local_heads, head_size)
    query = qkv[:, 0]
    keys = qkv[:, 1]
    values = qkv[:, 2]
    top = jnp.full((tok_rows, local_heads), -jnp.inf, jnp.float32)
    total = jnp.zeros((tok_rows, local_heads), jnp.float32)
    mixed = jnp.zeros((tok_rows, local_heads, head_size), jnp.float32)
    key_piece = lax.all_gather(keys, "seq", axis=0, tiled=True)
    value_piece = lax.all_gather(values, "seq", axis=0, tiled=True)
    block_scores = jnp.einsum(
        "thd,rhd->thr", query, key_piece, preferred_element_type=jnp.float32
    ) / math.sqrt(head_size)
    new_top = jnp.max(block_scores, axis=-1)
    scale = jnp.exp(top - new_top)
    weights = jnp.exp(block_scores - new_top[..., None])
    total = total * scale + jnp.sum(weights, axis=-1)
    update = jnp.einsum(
        "thr,rhd->thd",
        weights.astype(jnp.bfloat16),
        value_piece,
        preferred_element_type=jnp.float32,
    )
    mixed = mixed * scale[..., None] + update
    top, total, mixed = (new_top, total, mixed)
    attended = (mixed / total[..., None]).reshape(tok_rows, local_cols).astype(jnp.bfloat16)
    part = attended
    summed = lax.psum_scatter(
        jnp.dot(part, out_weight, preferred_element_type=jnp.float32).astype(jnp.bfloat16),
        "var",
        scatter_dimension=0,
        tiled=True,
    ).astype(jnp.float32)
    layer_part = (own_rows.astype(jnp.float32) + summed).astype(jnp.bfloat16)
    layer = lax.all_gather(layer_part, "var", axis=0, tiled=True)
    part = layer
    return lax.psum_scatter(
        lax.dot_general(
            part, head_cot, (((0,), (0,)), ((), ())), preferred_element_type=jnp.float32
        ).astype(jnp.bfloat16),
        "seq",
        scatter_dimension=0,
        tiled=True,
    ).astype(jnp.float32)


def solution(mesh):
    return jax.shard_map(
        body,
        mesh=mesh,
        in_specs=(
            P("var", "seq", None),
            P("var", None, None),
            P("var", None),
            P(),
            P(),
            P(None, None, "var"),
            P("var", None),
            P("seq", "var"),
        ),
        out_specs=P("seq", "var"),
        check_vma=False,
    )
```

profile of v0, /device:TPU:0, one launch (start us, length us, event | category | flops | bytes accessed | tf_op | source)
XLA Modules:
  0.0 341.9 jit_solution(12588068427211002149)
XLA Ops:
  8.5 2.7 add_convert_fusion
  11.2 4.3 %convert_bitcast_fusion.5 = (f32[16,8,32,128]{3,1,2,0:T(8,128)S(1)}, f32[16,8,32,128]{3,1,2,0:T(8,128)}, f32[16,8,32,128]{3,1,2,0:T(8,128)}, f32[16,8,32,128]{3,...) fusion(bf16[6,128,4096]{2,1,0:T(8,128)(2,1)S(1)} %add_convert_fusion), kind=kLoop, calls=%fused_computation.36 | loop fusion | flops 3145728 | bytes 18874368
  25.8 5.3 %fusion.8 = f32[1,128,32,128]{3,2,1,0:T(8,128)} fusion(f32[128,32]{1,0:T(8,128)S(1)} %copy.37, f32[128,32]{1,0:T(8,128)S(1)} %copy.36, f32[128,32]{1,0:T(8,128)S(1)} %copy.35, f32[128,32]{1,0:T(8,128)S(1)} %copy.34, f32[128,32]{1,0:T(8,128)S(1)} %copy.33, f32[128,32]{1,0:T(8,128)S(1)} %copy.32, f32[1,128,32,128]{3,2,1,0:T(8,128)S(1)} %bitcast.148, ...), kind=kLoop, calls=%fused_computation.20 | loop fusion | flops 5767168 | bytes 14778368 | tf_op jit(solution)/shard_map/add | solution.py:58
  31.2 10.8 %all-gather.1 = f32[1024,32]{0,1:T(8,128)S(1)} all-gather(f32[128,32]{0,1:T(8,128)S(1)} %get-tuple-element.211), channel_id=3, replica_groups=mesh['var'=8,'seq'=4] {'var'}, dimensions={0}, use_global_device_ids=true | all-gather | bytes 147456 | tf_op jit(solution)/shard_map/all_gather | solution.py:12
  42.2 10.2 %all-gather = f32[1024,32]{0,1:T(8,128)S(1)} all-gather(f32[128,32]{0,1:T(8,128)S(1)} %get-tuple-element.230), channel_id=2, replica_groups=mesh['var'=8,'seq'=4] {'var'}, dimensions={0}, use_global_device_ids=true | all-gather | bytes 147456 | tf_op jit(solution)/shard_map/all_gather | solution.py:12
  53.6 16.9 %copy.42 = bf16[4096,3,512]{0,2,1:T(8,128)(2,1)} copy(bf16[4096,3,512]{2,0,1:T(8,128)(2,1)} %param.15) | data formatting | bytes 25165824 | tf_op args[5]
  70.5 53.7 %all-gather.7.cloned.1.call-done = f32[8,128,32,128]{3,2,1,0:T(8,128)} async-done(((f32[1,128,32,128]{3,2,1,0:T(8,128)}), f32[8,128,32,128]{3,2,1,0:T(8,128)}) %all-gather.7.cloned.1.call-update) | async-done | bytes 16777232 | tf_op jit(solution)/shard_map/all_gather | solution.py:12
  126.0 32.9 %while.19 = (s32[]{:T(128)}, f32[128,32]{1,0:T(8,128)S(1)}, f32[128,32]{1,0:T(8,128)S(1)}, f32[128,32,128]{2,1,0:T(8,128)S(1)}, f32[8,128,32]{2,1,0:T(8,128)}, /...) while((s32[]{:T(128)}, f32[128,32]{1,0:T(8,128)S(1)}, ...), condition=%wide.region_3.0_spmd, body=%wide.region_2.0_spmd.sunk | while | flops 1597445 | bytes 6455447 | solution.py:18
  126.9 3.8 %fusion.43 = f32[128,32,128]{2,1,0:T(8,128)S(1)} fusion(f32[8,128,32,128]{3,2,1,0:T(8,128)} %get-tuple-element.311, s32[]{:T(128)S(6)} %select_n.17, f32[128,32,128]{2,1,0:T(8,128)S(1)} %get-tuple-element.298, f32[128,32]{1,0:T(8,128)S(1)} %get-tuple-element.283, f32[128,32]{1,0:T(8,128)S(1)} %get-tuple-element.284), kind=kLoop, calls=%fused_computation.1.clone.1 | loop fusion | flops 1572864 | bytes 6324228 | tf_op jit(solution)/shard_map/while/body/eval_jaxpr/add | solution.py:36
  131.6 3.8 %fusion.43 = f32[128,32,128]{2,1,0:T(8,128)S(1)} fusion(f32[8,128,32,128]{3,2,1,0:T(8,128)} %get-tuple-element.311, s32[]{:T(128)S(6)} %select_n.17, f32[128,32,128]{2,1,0:T(8,128)S(1)} %get-tuple-element.298, f32[128,32]{1,0:T(8,128)S(1)} %get-tuple-element.283, f32[128,32]{1,0:T(8,128)S(1)} %get-tuple-element.284), kind=kLoop, calls=%fused_computation.1.clone.1 | loop fusion | flops 1572864 | bytes 6324228 | tf_op jit(solution)/shard_map/while/body/eval_jaxpr/add | solution.py:36
  136.3 3.8 %fusion.43 = f32[128,32,128]{2,1,0:T(8,128)S(1)} fusion(f32[8,128,32,128]{3,2,1,0:T(8,128)} %get-tuple-element.311, s32[]{:T(128)S(6)} %select_n.17, f32[128,32,128]{2,1,0:T(8,128)S(1)} %get-tuple-element.298, f32[128,32]{1,0:T(8,128)S(1)} %get-tuple-element.283, f32[128,32]{1,0:T(8,128)S(1)} %get-tuple-element.284), kind=kLoop, calls=%fused_computation.1.clone.1 | loop fusion | flops 1572864 | bytes 6324228 | tf_op jit(solution)/shard_map/while/body/eval_jaxpr/add | solution.py:36
  141.0 3.8 %fusion.43 = f32[128,32,128]{2,1,0:T(8,128)S(1)} fusion(f32[8,128,32,128]{3,2,1,0:T(8,128)} %get-tuple-element.311, s32[]{:T(128)S(6)} %select_n.17, f32[128,32,128]{2,1,0:T(8,128)S(1)} %get-tuple-element.298, f32[128,32]{1,0:T(8,128)S(1)} %get-tuple-element.283, f32[128,32]{1,0:T(8,128)S(1)} %get-tuple-element.284), kind=kLoop, calls=%fused_computation.1.clone.1 | loop fusion | flops 1572864 | bytes 6324228 | tf_op jit(solution)/shard_map/while/body/eval_jaxpr/add | solution.py:36
  145.7 3.8 %fusion.43 = f32[128,32,128]{2,1,0:T(8,128)S(1)} fusion(f32[8,128,32,128]{3,2,1,0:T(8,128)} %get-tuple-element.311, s32[]{:T(128)S(6)} %select_n.17, f32[128,32,128]{2,1,0:T(8,128)S(1)} %get-tuple-element.298, f32[128,32]{1,0:T(8,128)S(1)} %get-tuple-element.283, f32[128,32]{1,0:T(8,128)S(1)} %get-tuple-element.284), kind=kLoop, calls=%fused_computation.1.clone.1 | loop fusion | flops 1572864 | bytes 6324228 | tf_op jit(solution)/shard_map/while/body/eval_jaxpr/add | solution.py:36
  150.4 3.8 %fusion.43 = f32[128,32,128]{2,1,0:T(8,128)S(1)} fusion(f32[8,128,32,128]{3,2,1,0:T(8,128)} %get-tuple-element.311, s32[]{:T(128)S(6)} %select_n.17, f32[128,32,128]{2,1,0:T(8,128)S(1)} %get-tuple-element.298, f32[128,32]{1,0:T(8,128)S(1)} %get-tuple-element.283, f32[128,32]{1,0:T(8,128)S(1)} %get-tuple-element.284), kind=kLoop, calls=%fused_computation.1.clone.1 | loop fusion | flops 1572864 | bytes 6324228 | tf_op jit(solution)/shard_map/while/body/eval_jaxpr/add | solution.py:36
  155.0 3.8 %fusion.43 = f32[128,32,128]{2,1,0:T(8,128)S(1)} fusion(f32[8,128,32,128]{3,2,1,0:T(8,128)} %get-tuple-element.311, s32[]{:T(128)S(6)} %select_n.17, f32[128,32,128]{2,1,0:T(8,128)S(1)} %get-tuple-element.298, f32[128,32]{1,0:T(8,128)S(1)} %get-tuple-element.283, f32[128,32]{1,0:T(8,128)S(1)} %get-tuple-element.284), kind=kLoop, calls=%fused_computation.1.clone.1 | loop fusion | flops 1572864 | bytes 6324228 | tf_op jit(solution)/shard_map/while/body/eval_jaxpr/add | solution.py:36
  163.3 8.9 %convolution_convert_fusion.2 = bf16[128,1536]{1,0:T(8,128)(2,1)S(1)} fusion(bf16[4096,1536]{0,1:T(8,128)(2,1)} %bitcast.146, bf16[16,8,32,128]{3,2,1,0:T(8,128)(2,1)S(1)} %bitcast.154), kind=kOutput, calls=%fused_computation.15 | convolution fusion | flops 1610809344 | bytes 14024704 | tf_op jit(solution)/shard_map/dot_general | solution.py:68
  172.4 16.1 %all-gather.2 = bf16[512,1,4,128]{3,0,2,1:T(8,128)(2,1)S(1)} all-gather(bf16[128,1,4,128]{3,0,2,1:T(8,128)(2,1)S(1)} %copy.50), channel_id=4, replica_groups=mesh['var'=8,'seq'=4] {'seq'}, dimensions={0}, use_global_device_ids=true | all-gather | bytes 655360 | tf_op jit(solution)/shard_map/all_gather | solution.py:78
  189.1 15.1 %all-gather.3 = bf16[512,1,4,128]{0,3,2,1:T(8,128)(2,1)S(1)} all-gather(bf16[128,1,4,128]{0,3,2,1:T(8,128)(2,1)S(1)} %copy.52), channel_id=5, replica_groups=mesh['var'=8,'seq'=4] {'seq'}, dimensions={0}, use_global_device_ids=true | all-gather | bytes 655360 | tf_op jit(solution)/shard_map/all_gather | solution.py:79
  204.5 3.9 %convolution_convert_fusion.1 = bf16[128,4096]{1,0:T(8,128)(2,1)} fusion(bf16[128,512]{0,1:T(8,128)(2,1)S(1)} %bitcast.158, bf16[512,4096]{1,0:T(8,128)(2,1)} %param.16), kind=kOutput, calls=%fused_computation.10 | convolution fusion | flops 537395200 | bytes 5373952 | tf_op jit(solution)/shard_map/dot_general | solution.py:98
  209.0 34.3 %reduce-scatter.3.cloned.1.call-done = bf16[16,4096]{1,0:T(8,128)(2,1)} async-done(((bf16[128,4096]{1,0:T(8,128)(2,1)}), bf16[16,4096]{1,0:T(8,128)(2,1)}) %reduce-scatter.3.cloned.1.call-update) | async-done | bytes 131088 | tf_op jit(solution)/shard_map/reduce_scatter | solution.py:97
  244.9 23.7 %all-gather.9.cloned.1.call-done = bf16[128,4096]{1,0:T(8,128)(2,1)} async-done(((bf16[16,4096]{1,0:T(8,128)(2,1)}), bf16[128,4096]{1,0:T(8,128)(2,1)}) %all-gather.9.cloned.1.call-update) | async-done | bytes 1048592 | tf_op jit(solution)/shard_map/all_gather | solution.py:104
  268.6 3.9 %convolution_convert_fusion = bf16[4096,384]{1,0:T(8,128)(2,1)} fusion(bf16[128,4096]{1,0:T(8,128)(2,1)} %all-gather.9.cloned.1.call-done, bf16[128,384]{1,0:T(8,128)(2,1)S(1)} %copy-done.7), kind=kOutput, calls=%fused_computation.9 | convolution fusion | flops 404226048 | bytes 4292608 | tf_op jit(solution)/shard_map/dot_general | solution.py:107
  272.6 60.4 %reduce-scatter.5.cloned.1.call-done = bf16[1024,384]{1,0:T(8,128)(2,1)} async-done(((bf16[4096,384]{1,0:T(8,128)(2,1)}), bf16[1024,384]{1,0:T(8,128)(2,1)}) %reduce-scatter.5.cloned.1.call-update) | async-done | bytes 786448 | tf_op jit(solution)/shard_map/reduce_scatter | solution.py:106
  333.0 2.4 convert_element_type.164
  (72 shorter events, 29.6 us)
Async XLA Ops:
  6.5 1.9 copy-start
  6.5 117.7 %all-gather.7.cloned.1.call-start = ((), (), s32[]{:S(2)}) async-start(), calls=%async_computation.2 | async-start | bytes 18874368 | tf_op jit(solution)/shard_map/all_gather | solution.py:12
  11.2 4.3 %copy-start.6 = (bf16[4096,32]{0,1:T(8,128)(2,1)S(1)}, bf16[4096,32]{0,1:T(8,128)(2,1)}, u32[]{:S(2)}) copy-start(bf16[4096,32]{0,1:T(8,128)(2,1)} %param.13) | copy-start | bytes 786436
  18.1 2.2 copy-start.5
  20.3 1.6 copy-start.4
  21.9 1.6 copy-start.3
  23.5 1.6 copy-start.2
  31.1 212.1 %reduce-scatter.3.cloned.1.call-start = ((), (), s32[]{:S(2)}) async-start(), calls=%async_computation.3 | async-start | bytes 1179648 | tf_op jit(solution)/shard_map/reduce_scatter | solution.py:97
  53.5 16.9 %copy-start.8 = (bf16[4096]{0:T(1024)(128)(2,1)S(1)}, bf16[4096]{0:T(1024)(128)(2,1)}, u32[]{:S(2)}) copy-start(bf16[4096]{0:T(1024)(128)(2,1)} %param.14) | copy-start | bytes 24580
  208.4 60.2 %copy-start.7 = (bf16[128,384]{1,0:T(8,128)(2,1)S(1)}, bf16[128,384]{1,0:T(8,128)(2,1)}, u32[]{:S(2)}) copy-start(bf16[128,384]{1,0:T(8,128)(2,1)} %param.17) | copy-start | bytes 294916
  208.5 60.2 %all-gather.9.cloned.1.call-start = ((), (), s32[]{:S(2)}) async-start(), calls=%async_computation.4 | async-start | bytes 1179648 | tf_op jit(solution)/shard_map/all_gather | solution.py:104
  244.9 88.1 %reduce-scatter.5.cloned.1.call-start = ((), (), s32[]{:S(2)}) async-start(), calls=%async_computation.5 | async-start | bytes 3932160 | tf_op jit(solution)/shard_map/reduce_scatter | solution.py:106
  272.5 62.8 %copy-start.1 = (bf16[6,64,4096]{2,1,0:T(8,128)(2,1)S(1)}, bf16[6,64,4096]{2,1,0:T(8,128)(2,1)}, u32[]{:S(2)}) copy-start(bf16[6,64,4096]{2,1,0:T(8,128)(2,1)} %param.11) | copy-start | bytes 9437188
Sparse Core Ops, SparseCore 0:
  31.3 92.8 all-gather.6
  208.6 34.6 reduce-scatter.2
  245.1 23.4 all-gather.8
  272.7 60.2 reduce-scatter.4
where the time goes:
time: 344 us; the launch traced here: 342 us
  waiting for transfers between devices  172 us (50%)
  blocking collectives  52.1 us (15%)
  other arithmetic  51.8 us (15%)
  local copies, waits for them, and re-layouts  30.1 us (9%)
  matrix products  22 us (6%)
  between operations  13.3 us (4%)
    reduce_scatter x1, waiting for transfers between devices, body(): lax.psum_scatter(lax.dot_general(part, head_cot, (((0,), (0,)), ((), ()))...  60.4 us
    all_gather x1, waiting for transfers between devices, merged(): everything = jax.tree.map(lambda part: lax.all_gather(part, axis), array)  53.7 us
    reduce_scatter x1, waiting for transfers between devices, body(): lax.psum_scatter(jnp.dot(part, out_weight, preferred_element_type=jnp.flo...  34.3 us
    add x7, other arithmetic, combine_parts(): numer = numer_a * scale_a[..., None] + numer_b * scale_b[..., None]  26.3 us
    unnamed x28, local copies, waits for them, and re-layouts  26.2 us
    all_gather x1, waiting for transfers between devices, body(): layer = lax.all_gather(layer_part, 'var', axis=0, tiled=True)  23.7 us
    all_gather x2, blocking collectives, merged(): everything = jax.tree.map(lambda part: lax.all_gather(part, axis), array)  20.9 us
    all_gather x1, blocking collectives, body(): key_piece = lax.all_gather(keys, 'seq', axis=0, tiled=True)  16.1 us
  transfers between devices with their start and end apart: 4, of which 4 were waited for; matrix products, arithmetic and copies ran while one was open for 5% of the time, Pallas kernels for 0%

commit v1 on v0

v1 whole, which is shorter than its diff:
```python
import functools
import math

import jax
import jax.numpy as jnp
from jax import lax
from jax.experimental import pallas as pl
from jax.experimental.pallas import tpu as pltpu
from jax.sharding import PartitionSpec as P

MESH = pl.DeviceIdType.MESH
F32 = jnp.float32
BF16 = jnp.bfloat16
eps = 1e-05
HD = 128


def dot(a, b, contract=((1,), (0,))):
    return lax.dot_general(a, b, (contract, ((), ())), preferred_element_type=F32)


def kernel(
    nv, ns,
    patches, pw_hbm, var_embed, query_map, gain, wqkv_hbm, wo_hbm, cot,
    gathered, cot_all,
    pw, wqkv, wo, emb, stats_own, stats_in, numer, factor, pair_in, pair_sum, chip_in,
    agg, normed, keys_own, values_own, keys_in, values_in, query, attended,
    part, pair_in2, pair_sum2, chip_in2, layer,
    local_sem, cot_send, cot_recv, stats_send, stats_recv, pair_send, pair_recv, chip_send, chip_recv,
    norm_send, norm_recv, norm_fsend, norm_frecv, key_send, key_recv, value_send, value_recv,
    pair2_send, pair2_recv, chip2_send, chip2_recv, layer_send, layer_recv,
    last_send, last_recv, last_fsend, last_frecv,
):
    count, _, rows = patches.shape
    width = pw.shape[2]
    heads = width // HD
    nch = nv // 2
    share = rows // nv
    cols = wo.shape[0]
    piece = width // ns
    me = lax.axis_index("var")
    band = lax.axis_index("seq")
    chip = me // 2
    core = me % 2
    mate = chip * 2 + (1 - core)
    order = list(range(1, nch)) + [0]
    pending = []

    def chip_at(k):
        return (chip + k) % nch

    def chip_from(k):
        return (chip + nch - k) % nch

    def send(src, dst, ssem, rsem, **target):
        copy = pltpu.make_async_remote_copy(
            src_ref=src, dst_ref=dst, send_sem=ssem, recv_sem=rsem, device_id=target, device_id_type=MESH
        )
        copy.start()
        pending.append(copy)
        return copy

    loads = [
        pltpu.make_async_copy(pw_hbm, pw, local_sem.at[0]),
        pltpu.make_async_copy(wqkv_hbm, wqkv, local_sem.at[1]),
        pltpu.make_async_copy(wo_hbm, wo, local_sem.at[2]),
    ]
    for load in loads:
        load.start()

    barrier = pltpu.get_barrier_semaphore()
    for k in range(1, nv):
        pl.semaphore_signal(barrier, inc=1, device_id={"var": (me + k) % nv}, device_id_type=MESH)
    for k in range(1, ns):
        pl.semaphore_signal(barrier, inc=1, device_id={"seq": (band + k) % ns}, device_id_type=MESH)

    loads[0].wait()
    tile = 512

    @pl.loop(0, width // tile)
    def _(t):
        at = pl.ds(pl.multiple_of(t * tile, tile), tile)
        for v in range(count):
            e = dot(patches[v], pw[v, :, at], ((0,), (0,)))
            emb[v, :, at] = (e + var_embed[v : v + 1, at].astype(F32)).astype(BF16)

    scores = [dot(query_map[...], emb[v], ((1,), (1,))) / math.sqrt(HD) for v in range(count)]
    peak = functools.reduce(jnp.maximum, scores)
    weights = [jnp.exp(s - peak) for s in scores]
    total = functools.reduce(jnp.add, weights)
    stats_own[0] = peak
    stats_own[1] = total

    pl.semaphore_wait(barrier, nv - 1 + ns - 1)
    stats = [
        send(stats_own, stats_in.at[k - 1], stats_send.at[k - 1], stats_recv.at[k - 1], var=(me + k) % nv)
        for k in range(1, nv)
    ]
    cots = [
        send(cot, cot_all.at[band], cot_send.at[k - 1], cot_recv.at[k - 1], seq=(band + k) % ns)
        for k in range(1, ns)
    ]
    cot_all[band] = cot[...]

    weights = [jnp.transpose(w) for w in weights]
    for h in range(heads):
        at = slice(h * HD, (h + 1) * HD)
        acc = weights[0][:, h : h + 1] * emb[0, :, at].astype(F32)
        for v in range(1, count):
            acc = acc + weights[v][:, h : h + 1] * emb[v, :, at].astype(F32)
        for d in range(nv):
            numer[d % 2, d // 2, :, at] = acc[d * share : (d + 1) * share]

    for copy in stats:
        copy.wait_recv()
    own_peak = stats_own[0]
    top = own_peak
    for k in range(nv - 1):
        top = jnp.maximum(top, stats_in[k, 0])
    whole = stats_own[1] * jnp.exp(own_peak - top)
    for k in range(nv - 1):
        whole = whole + stats_in[k, 1] * jnp.exp(stats_in[k, 0] - top)
    scale = jnp.transpose(jnp.exp(own_peak - top) / whole)
    for d in range(nv):
        factor[d % 2, d // 2] = scale[d * share : (d + 1) * share]

    def scaled(c, j, h):
        return numer[c, j, :, h * HD : (h + 1) * HD] * factor[c, j, :, h : h + 1]

    pairs = []
    for i, k in enumerate(order):
        j = chip_at(k)
        for h in range(heads):
            numer[1 - core, j, :, h * HD : (h + 1) * HD] = scaled(1 - core, j, h)
        pairs.append(
            send(numer.at[1 - core, j], pair_in.at[i], pair_send.at[i], pair_recv.at[i], var=mate)
        )
    chips = []
    for i, k in enumerate(order):
        j = chip_at(k)
        pairs[i].wait_recv()
        for h in range(heads):
            at = slice(h * HD, (h + 1) * HD)
            pair_sum[i, :, at] = scaled(core, j, h) + pair_in[i, :, at]
        if k:
            chips.append(
                send(pair_sum.at[i], chip_in.at[i], chip_send.at[i], chip_recv.at[i], var=2 * j + core)
            )
    for copy in chips:
        copy.wait_recv()
    sums = pair_sum[nch - 1]
    for i in range(nch - 1):
        sums = sums + chip_in[i]
    own = sums.astype(BF16)
    agg[...] = own

    own = own.astype(F32)
    center = jnp.mean(own, axis=-1, keepdims=True)
    shifted = own - center
    spread = jnp.mean(shifted * shifted, axis=-1, keepdims=True)
    normed[me] = (shifted * lax.rsqrt(spread + eps) * gain[...].astype(F32)).astype(BF16)

    def gather(part_of, ssem, rsem, fsend, frecv):
        mine = part_of(me)
        direct = [
            send(mine, mine, ssem.at[k - 1], rsem.at[k - 1], var=2 * chip_at(k) + core) for k in range(1, nch)
        ]
        across = [send(mine, mine, fsend.at[0], frecv.at[0], var=mate)]
        for k in range(1, nch):
            direct[k - 1].wait_recv()
            got = part_of(2 * chip_from(k) + core)
            across.append(send(got, got, fsend.at[k], frecv.at[k], var=mate))
        for copy in across:
            copy.wait_recv()

    gather(lambda d: normed.at[d], norm_send, norm_recv, norm_fsend, norm_frecv)

    step = 256
    loads[1].wait()

    def project(which, out):
        @pl.loop(0, cols // step)
        def _(t):
            at = pl.ds(pl.multiple_of(t * step, step), step)
            out[:, at] = dot(normed[...].reshape(rows, width), wqkv[which, :, at]).astype(BF16)

    project(1, keys_own)
    key_copies = [
        send(keys_own, keys_in.at[k - 1], key_send.at[k - 1], key_recv.at[k - 1], seq=(band + k) % ns)
        for k in range(1, ns)
    ]
    project(2, values_own)
    value_copies = [
        send(values_own, values_in.at[k - 1], value_send.at[k - 1], value_recv.at[k - 1], seq=(band + k) % ns)
        for k in range(1, ns)
    ]
    project(0, query)
    for copy in key_copies:
        copy.wait_recv()
    probs, totals = [], []
    for h in range(cols // HD):
        at = slice(h * HD, (h + 1) * HD)
        q = query[:, at]
        blocks = [dot(q, keys_own[:, at], ((1,), (1,)))]
        blocks += [dot(q, keys_in[k, :, at], ((1,), (1,))) for k in range(ns - 1)]
        s = jnp.concatenate(blocks, axis=1) / math.sqrt(HD)
        e = jnp.exp(s - jnp.max(s, axis=-1, keepdims=True))
        totals.append(jnp.sum(e, axis=-1, keepdims=True))
        probs.append(e.astype(BF16))
    for copy in value_copies:
        copy.wait_recv()
    for h in range(cols // HD):
        at = slice(h * HD, (h + 1) * HD)
        vals = jnp.concatenate([values_own[:, at]] + [values_in[k, :, at] for k in range(ns - 1)], axis=0)
        attended[:, at] = (dot(probs[h], vals) / totals[h]).astype(BF16)

    loads[2].wait()

    @pl.loop(0, width // tile)
    def _(t):
        at = pl.ds(pl.multiple_of(t * tile, tile), tile)
        p = dot(attended[...], wo[:, at])
        for d in range(nv):
            part[d % 2, d // 2, :, at] = p[d * share : (d + 1) * share]

    pairs = [
        send(part.at[1 - core, chip_at(k)], pair_in2.at[i], pair2_send.at[i], pair2_recv.at[i], var=mate)
        for i, k in enumerate(order)
    ]
    chips = []
    for i, k in enumerate(order):
        j = chip_at(k)
        pairs[i].wait_recv()
        if k:
            pair_sum2[i] = (part[core, j] + pair_in2[i]).astype(BF16)
            chips.append(
                send(pair_sum2.at[i], chip_in2.at[i], chip2_send.at[i], chip2_recv.at[i], var=2 * j + core)
            )
    sums = agg[...].astype(F32) + (part[core, chip] + pair_in2[nch - 1])
    for i in range(nch - 1):
        chips[i].wait_recv()
        sums = sums + chip_in2[i].astype(F32)
    sums = sums.astype(BF16)
    for s in range(ns):
        layer[s] = sums[:, s * piece : (s + 1) * piece]

    copies = [
        send(
            layer.at[(band + k) % ns], gathered.at[band, me], layer_send.at[k - 1], layer_recv.at[k - 1],
            seq=(band + k) % ns,
        )
        for k in range(1, ns)
    ]
    gathered[band, me] = layer[band]
    for copy in copies:
        copy.wait_recv()
    gather(lambda d: gathered.at[:, d], last_send, last_recv, last_fsend, last_frecv)
    for copy in cots:
        copy.wait_recv()
    for copy in pending:
        copy.wait_send()


def body(nv, ns, patches, patch_weight, var_embed, agg_query, norm_gain, qkv_weight, out_weight, head_cot):
    count, rows, pixels = patches.shape
    width = patch_weight.shape[2]
    heads = agg_query.shape[1]
    cols = out_weight.shape[0]
    share = rows // nv
    nch = nv // 2
    piece = width // ns
    dma = pltpu.SemaphoreType.DMA
    vmem = pl.BlockSpec(memory_space=pltpu.VMEM)
    anywhere = pl.BlockSpec(memory_space=pl.ANY)
    V = pltpu.VMEM
    gathered, cot_all = pl.pallas_call(
        functools.partial(kernel, nv, ns),
        out_shape=[
            jax.ShapeDtypeStruct((ns, nv, share, piece), BF16),
            jax.ShapeDtypeStruct((ns,) + head_cot.shape, BF16),
        ],
        in_specs=[vmem, anywhere, vmem, vmem, vmem, anywhere, anywhere, vmem],
        out_specs=[vmem, vmem],
        scratch_shapes=[
            V((count, pixels, width), BF16),
            V((3, width, cols), BF16),
            V((cols, width), BF16),
            V((count, rows, width), BF16),
            V((2, heads, rows), F32),
            V((nv - 1, 2, heads, rows), F32),
            V((2, nch, share, width), F32),
            V((2, nch, share, heads), F32),
            V((nch, share, width), F32),
            V((nch, share, width), F32),
            V((nch - 1, share, width), F32),
            V((share, width), BF16),
            V((nv, share, width), BF16),
            V((rows, cols), BF16),
            V((rows, cols), BF16),
            V((ns - 1, rows, cols), BF16),
            V((ns - 1, rows, cols), BF16),
            V((rows, cols), BF16),
            V((rows, cols), BF16),
            V((2, nch, share, width), F32),
            V((nch, share, width), F32),
            V((nch - 1, share, width), BF16),
            V((nch - 1, share, width), BF16),
            V((ns, share, piece), BF16),
            dma((3,)),
            dma((ns - 1,)), dma((ns - 1,)),
            dma((nv - 1,)), dma((nv - 1,)),
            dma((nch,)), dma((nch,)),
            dma((nch - 1,)), dma((nch - 1,)),
            dma((nch - 1,)), dma((nch - 1,)), dma((nch,)), dma((nch,)),
            dma((ns - 1,)), dma((ns - 1,)), dma((ns - 1,)), dma((ns - 1,)),
            dma((nch,)), dma((nch,)),
            dma((nch - 1,)), dma((nch - 1,)),
            dma((ns - 1,)), dma((ns - 1,)),
            dma((nch - 1,)), dma((nch - 1,)), dma((nch,)), dma((nch,)),
        ],
        compiler_params=pltpu.CompilerParams(
            collective_id=0, has_side_effects=True, vmem_limit_bytes=56 * 1024 * 1024
        ),
    )(
        jnp.transpose(patches, (0, 2, 1)),
        patch_weight,
        var_embed,
        jnp.transpose(agg_query),
        norm_gain.reshape(1, width),
        jnp.transpose(qkv_weight, (1, 0, 2)),
        out_weight,
        head_cot,
    )
    tokens = ns * rows
    return lax.dot_general(
        gathered.reshape(tokens, piece),
        cot_all.reshape(tokens, head_cot.shape[1]),
        (((0,), (0,)), ((), ())),
        preferred_element_type=F32,
    )


def solution(mesh):
    nv, ns = mesh.shape["var"], mesh.shape["seq"]
    return jax.shard_map(
        functools.partial(body, nv, ns),
        mesh=mesh,
        in_specs=(
            P("var", "seq", None),
            P("var", None, None),
            P("var", None),
            P(),
            P(),
            P(None, None, "var"),
            P("var", None),
            P("seq", "var"),
        ),
        out_specs=P("seq", "var"),
        check_vma=False,
    )
```

time: 344 us -> 95.1 us (0.28)
  waiting for transfers between devices: 172 us -> 0 us
  Pallas kernels: 0 us -> 90.3 us
  blocking collectives: 52.1 us -> 0 us
  other arithmetic: 51.8 us -> 0 us
  local copies, waits for them, and re-layouts: 30.1 us -> 1.31 us
  matrix products: 22 us -> 3.2 us
  between operations: 13.3 us -> 0.01 us
    reduce_scatter x2 -> x0, waiting for transfers between devices: 94.7 us -> none  [the longest x1 60.4 us: body(): lax.psum_scatter(lax.dot_general(part, head_cot, (((0,), (0,)), ((), ()))...]
    pallas_call x0 -> x1, Pallas kernels: none -> 90.3 us  [body(): pl.pallas_call(functools.partial(kernel, nv, ns), out_shape=[jax.ShapeDty...]
    all_gather x2 -> x0, waiting for transfers between devices: 77.5 us -> none  [the longest x1 53.7 us: merged(): everything = jax.tree.map(lambda part: lax.all_gather(part, axis), array)]
    all_gather x4 -> x0, blocking collectives: 52.1 us -> none  [the longest x2 20.9 us: merged(): everything = jax.tree.map(lambda part: lax.all_gather(part, axis), array)]
    add x15 -> x0, other arithmetic: 37.9 us -> none  [the longest x7 26.3 us: combine_parts(): numer = numer_a * scale_a[..., None] + numer_b * scale_b[..., None]]
    unnamed x28 -> x0, local copies, waits for them, and re-layouts: 26.2 us -> none
    dot_general x7 -> x1, matrix products: 22 us -> 3.2 us  [body(): lax.dot_general(gathered.reshape(tokens, piece), cot_all.reshape(tokens,...]
    convert_element_type x4 -> x0, other arithmetic: 5.39 us -> none  [the longest x1 2.38 us: body(): return lax.psum_scatter(lax.dot_general(part, head_cot, (((0,), (0,)), ((...]
  transfers between devices with their start and end apart: 4 -> 0, of which waited for: 4 -> 0; matrix products, arithmetic and copies ran while one was open for 5% -> 0% of each run, Pallas kernels for 0% -> 0%
where the time goes in v1:
time: 95.1 us; the launch traced here: 94.9 us
  Pallas kernels  90.3 us (95%)
  matrix products  3.2 us (3%)
  local copies, waits for them, and re-layouts  1.31 us (1%)
    pallas_call x1, Pallas kernels, body(): pl.pallas_call(functools.partial(kernel, nv, ns), out_shape=[jax.ShapeDty...  90.3 us
    dot_general x1, matrix products, body(): lax.dot_general(gathered.reshape(tokens, piece), cot_all.reshape(tokens,...  3.2 us

profile of v1, /device:TPU:0, one launch (start us, length us, event | category | flops | bytes accessed | tf_op | source)
XLA Modules:
  0.0 94.9 jit_solution(3732974640706991834)
XLA Ops:
  0.0 1.3 %reshape.9.gain = bf16[1,4096]{1,0:T(2,128)(2,1)} reshape(bf16[4096]{0:T(1024)(128)(2,1)} %param.12) | data formatting | bytes 16384 | tf_op jit(solution)/shard_map/reshape | solution.py:329
  1.3 90.3 %shard_map.82 = (bf16[4,8,16,1024]{3,2,1,0:T(8,128)(2,1)}, bf16[4,128,384]{2,1,0:T(8,128)(2,1)}) custom-call(bf16[6,64,128]{2,1,0:T(8,128)(2,1)} %bitcast.11, bf16[6,64,4096]{2,1,0:T(8,128)(2,1)} %pw_hbm.1, bf16[6,4096]{1,0:T(8,128)(2,1)} %var_embed.1, bf16[32,4096]{1,0:T(8,128)(2,1)} %bitcast.10, bf16[1,4096]{1,0:T(2,128)(2,1)} %reshape.9.gain, ...), custom_call_target="tpu_custom_call" | custom-call | tf_op jit(solution)/shard_map/pallas_call | solution.py:276
  91.7 3.2 %fusion = f32[1024,384]{1,0:T(8,128)} fusion(bf16[512,1024]{1,0:T(8,128)(2,1)} %bitcast.8, bf16[512,384]{1,0:T(8,128)(2,1)} %bitcast.9), kind=kOutput, calls=%fused_computation | convolution fusion | flops 402653184 | bytes 3014656 | tf_op jit(solution)/shard_map/dot_general | solution.py:335

commit v2 on v1

--- a/solution.py
+++ b/solution.py
@@ -23,11 +23,12 @@
     nv, ns,
     patches, pw_hbm, var_embed, query_map, gain, wqkv_hbm, wo_hbm, cot,
     gathered, cot_all,
-    pw, wqkv, wo, emb, stats_own, stats_in, numer, factor, pair_in, pair_sum, chip_in,
-    agg, normed, keys_own, values_own, keys_in, values_in, query, attended,
+    pw, wqkv, wo, emb, weights, stats_own, stats_in, for_mate, factor, pair_in, pair_sum, chip_in,
+    agg, normed, keys_own, values_own, query_own, keys_in, values_in, query_in, mixed, attended,
     part, pair_in2, pair_sum2, chip_in2, layer,
-    local_sem, cot_send, cot_recv, stats_send, stats_recv, pair_send, pair_recv, chip_send, chip_recv,
+    pw_sem, local_sem, cot_send, cot_recv, stats_send, stats_recv, pair_send, pair_recv, chip_send, chip_recv,
     norm_send, norm_recv, norm_fsend, norm_frecv, key_send, key_recv, value_send, value_recv,
+    query_send, query_recv, mixed_send, mixed_recv,
     pair2_send, pair2_recv, chip2_send, chip2_recv, layer_send, layer_recv,
     last_send, last_recv, last_fsend, last_frecv,
 ):
@@ -38,6 +39,8 @@
     share = rows // nv
     cols = wo.shape[0]
     piece = width // ns
+    spread_heads = cols // HD % ns == 0
+    groups, _, gcols = attended.shape
     me = lax.axis_index("var")
     band = lax.axis_index("seq")
     chip = me // 2
@@ -60,13 +63,13 @@
         pending.append(copy)
         return copy
 
+    embed_loads = [pltpu.make_async_copy(pw_hbm.at[v], pw.at[v], pw_sem.at[v]) for v in range(count)]
+    for load in embed_loads:
+        load.start()
     loads = [
-        pltpu.make_async_copy(pw_hbm, pw, local_sem.at[0]),
-        pltpu.make_async_copy(wqkv_hbm, wqkv, local_sem.at[1]),
-        pltpu.make_async_copy(wo_hbm, wo, local_sem.at[2]),
+        pltpu.make_async_copy(wqkv_hbm, wqkv, local_sem.at[0]),
+        pltpu.make_async_copy(wo_hbm, wo, local_sem.at[1]),
     ]
-    for load in loads:
-        load.start()
 
     barrier = pltpu.get_barrier_semaphore()
     for k in range(1, nv):
@@ -74,20 +77,26 @@
     for k in range(1, ns):
         pl.semaphore_signal(barrier, inc=1, device_id={"seq": (band + k) % ns}, device_id_type=MESH)
 
-    loads[0].wait()
     tile = 512
-
-    @pl.loop(0, width // tile)
-    def _(t):
-        at = pl.ds(pl.multiple_of(t * tile, tile), tile)
-        for v in range(count):
-            e = dot(patches[v], pw[v, :, at], ((0,), (0,)))
-            emb[v, :, at] = (e + var_embed[v : v + 1, at].astype(F32)).astype(BF16)
-
-    scores = [dot(query_map[...], emb[v], ((1,), (1,))) / math.sqrt(HD) for v in range(count)]
+    scores = []
+    for v in range(count):
+        embed_loads[v].wait()
+        if v == count - 1:
+            for load in loads:
+                load.start()
+        pixels = jnp.transpose(patches[v])
+
+        @pl.loop(0, width // tile)
+        def _(t):
+            at = pl.ds(pl.multiple_of(t * tile, tile), tile)
+            e = (dot(pixels, pw[v, :, at]) + var_embed[v : v + 1, at].astype(F32)).astype(BF16)
+            for d in range(nv):
+                emb[v, d, :, at] = e[d * share : (d + 1) * share]
+
+        scores.append(dot(query_map[...], emb[v].reshape(rows, width), ((1,), (1,))) / math.sqrt(HD))
     peak = functools.reduce(jnp.maximum, scores)
-    weights = [jnp.exp(s - peak) for s in scores]
-    total = functools.reduce(jnp.add, weights)
+    unscaled = [jnp.exp(s - peak) for s in scores]
+    total = functools.reduce(jnp.add, unscaled)
     stats_own[0] = peak
     stats_own[1] = total
 
@@ -102,14 +111,25 @@
     ]
     cot_all[band] = cot[...]
 
-    weights = [jnp.transpose(w) for w in weights]
-    for h in range(heads):
-        at = slice(h * HD, (h + 1) * HD)
-        acc = weights[0][:, h : h + 1] * emb[0, :, at].astype(F32)
-        for v in range(1, count):
-            acc = acc + weights[v][:, h : h + 1] * emb[v, :, at].astype(F32)
+    for v in range(count):
+        w = jnp.transpose(unscaled[v])
         for d in range(nv):
-            numer[d % 2, d // 2, :, at] = acc[d * share : (d + 1) * share]
+            weights[v, d] = w[d * share : (d + 1) * share]
+
+    def weighted(d):
+        w = [weights[v, d] for v in range(count)]
+        for h in range(heads):
+            at = slice(h * HD, (h + 1) * HD)
+            acc = w[0][:, h : h + 1] * emb[0, d, :, at].astype(F32)
+            for v in range(1, count):
+                acc = acc + w[v][:, h : h + 1] * emb[v, d, :, at].astype(F32)
+            yield h, at, acc
+
+    pairs = []
+    for i, k in enumerate(order):
+        for h, at, acc in weighted(2 * chip_at(k) + 1 - core):
+            for_mate[i, :, at] = acc
+        pairs.append(send(for_mate.at[i], pair_in.at[i], pair_send.at[i], pair_recv.at[i], var=mate))
 
     for copy in stats:
         copy.wait_recv()
@@ -120,32 +140,21 @@
     whole = stats_own[1] * jnp.exp(own_peak - top)
     for k in range(nv - 1):
         whole = whole + stats_in[k, 1] * jnp.exp(stats_in[k, 0] - top)
-    scale = jnp.transpose(jnp.exp(own_peak - top) / whole)
-    for d in range(nv):
-        factor[d % 2, d // 2] = scale[d * share : (d + 1) * share]
-
-    def scaled(c, j, h):
-        return numer[c, j, :, h * HD : (h + 1) * HD] * factor[c, j, :, h : h + 1]
-
-    pairs = []
-    for i, k in enumerate(order):
-        j = chip_at(k)
-        for h in range(heads):
-            numer[1 - core, j, :, h * HD : (h + 1) * HD] = scaled(1 - core, j, h)
-        pairs.append(
-            send(numer.at[1 - core, j], pair_in.at[i], pair_send.at[i], pair_recv.at[i], var=mate)
-        )
+    mate_peak = stats_in[(1 - core) * (nv - 2), 0]
+    for which, part_peak in enumerate((own_peak, mate_peak)):
+        scale = jnp.transpose(jnp.exp(part_peak - top) / whole)
+        for d in range(nv):
+            factor[which, d] = scale[d * share : (d + 1) * share]
+
     chips = []
     for i, k in enumerate(order):
-        j = chip_at(k)
+        d = 2 * chip_at(k) + core
+        own_factor, mate_factor = factor[0, d], factor[1, d]
         pairs[i].wait_recv()
-        for h in range(heads):
-            at = slice(h * HD, (h + 1) * HD)
-            pair_sum[i, :, at] = scaled(core, j, h) + pair_in[i, :, at]
+        for h, at, acc in weighted(d):
+            pair_sum[i, :, at] = acc * own_factor[:, h : h + 1] + pair_in[i, :, at] * mate_factor[:, h : h + 1]
         if k:
-            chips.append(
-                send(pair_sum.at[i], chip_in.at[i], chip_send.at[i], chip_recv.at[i], var=2 * j + core)
-            )
+            chips.append(send(pair_sum.at[i], chip_in.at[i], chip_send.at[i], chip_recv.at[i], var=d))
     for copy in chips:
         copy.wait_recv()
     sums = pair_sum[nch - 1]
@@ -158,7 +167,7 @@
     center = jnp.mean(own, axis=-1, keepdims=True)
     shifted = own - center
     spread = jnp.mean(shifted * shifted, axis=-1, keepdims=True)
-    normed[me] = (shifted * lax.rsqrt(spread + eps) * gain[...].astype(F32)).astype(BF16)
+    normed[me] = (shifted * lax.rsqrt(spread + eps) * gain[...].astype(F32)[None, :]).astype(BF16)
 
     def gather(part_of, ssem, rsem, fsend, frecv):
         mine = part_of(me)
@@ -176,50 +185,77 @@
     gather(lambda d: normed.at[d], norm_send, norm_recv, norm_fsend, norm_frecv)
 
     step = 256
+    loads[0].wait()
+
+    def plane(k):
+        return (band + k) % ns if spread_heads else 0
+
+    def project(which, out):
+        for t in range(cols // step):
+            p = dot(normed[...].reshape(rows, width), wqkv[which, :, t * step : (t + 1) * step]).astype(BF16)
+            span = min(step, gcols)
+            for c in range(0, step, span):
+                at = t * step + c
+                out[at // gcols, :, at % gcols : at % gcols + span] = p[:, c : c + span]
+
+    def to_bands(own, landing, ssem, rsem):
+        return [
+            send(own.at[plane(k)], landing.at[k - 1], ssem.at[k - 1], rsem.at[k - 1], seq=(band + k) % ns)
+            for k in range(1, ns)
+        ]
+
+    project(1, keys_own)
+    copies = to_bands(keys_own, keys_in, key_send, key_recv)
+    project(0, query_own)
+    if spread_heads:
+        copies += to_bands(query_own, query_in, query_send, query_recv)
+    project(2, values_own)
+    value_copies = to_bands(values_own, values_in, value_send, value_recv)
+    for copy in copies:
+        copy.wait_recv()
+
+    def all_rows(own, landing, at):
+        return jnp.concatenate([own[plane(0), :, at]] + [landing[k, :, at] for k in range(ns - 1)], axis=0)
+
+    sources = list(range(1, ns)) + [0] if spread_heads else [0]
+    ready = {}
+    for h in range(gcols // HD):
+        at = slice(h * HD, (h + 1) * HD)
+        keys = all_rows(keys_own, keys_in, at)
+        for k in sources:
+            q = query_in[k - 1, :, at] if k else query_own[plane(0), :, at]
+            s = dot(q, keys, ((1,), (1,))) / math.sqrt(HD)
+            e = jnp.exp(s - jnp.max(s, axis=-1, keepdims=True))
+            ready[h, k] = e.astype(BF16), jnp.sum(e, axis=-1, keepdims=True)
+    for copy in value_copies:
+        copy.wait_recv()
+    copies = []
+    for k in sources:
+        for h in range(gcols // HD):
+            at = slice(h * HD, (h + 1) * HD)
+            probs, total = ready[h, k]
+            out = (dot(probs, all_rows(values_own, values_in, at)) / total).astype(BF16)
+            if k:
+                mixed[k - 1, :, at] = out
+            else:
+                attended[plane(0), :, at] = out
+        if k:
+            copies.append(
+                send(
+                    mixed.at[k - 1], attended.at[band], mixed_send.at[k - 1], mixed_recv.at[k - 1],
+                    seq=(band + ns - k) % ns,
+                )
+            )
+    for copy in copies:
+        copy.wait_recv()
+
     loads[1].wait()
-
-    def project(which, out):
-        @pl.loop(0, cols // step)
-        def _(t):
-            at = pl.ds(pl.multiple_of(t * step, step), step)
-            out[:, at] = dot(normed[...].reshape(rows, width), wqkv[which, :, at]).astype(BF16)
-
-    project(1, keys_own)
-    key_copies = [
-        send(keys_own, keys_in.at[k - 1], key_send.at[k - 1], key_recv.at[k - 1], seq=(band + k) % ns)
-        for k in range(1, ns)
-    ]
-    project(2, values_own)
-    value_copies = [
-        send(values_own, values_in.at[k - 1], value_send.at[k - 1], value_recv.at[k - 1], seq=(band + k) % ns)
-        for k in range(1, ns)
-    ]
-    project(0, query)
-    for copy in key_copies:
-        copy.wait_recv()
-    probs, totals = [], []
-    for h in range(cols // HD):
-        at = slice(h * HD, (h + 1) * HD)
-        q = query[:, at]
-        blocks = [dot(q, keys_own[:, at], ((1,), (1,)))]
-        blocks += [dot(q, keys_in[k, :, at], ((1,), (1,))) for k in range(ns - 1)]
-        s = jnp.concatenate(blocks, axis=1) / math.sqrt(HD)
-        e = jnp.exp(s - jnp.max(s, axis=-1, keepdims=True))
-        totals.append(jnp.sum(e, axis=-1, keepdims=True))
-        probs.append(e.astype(BF16))
-    for copy in value_copies:
-        copy.wait_recv()
-    for h in range(cols // HD):
-        at = slice(h * HD, (h + 1) * HD)
-        vals = jnp.concatenate([values_own[:, at]] + [values_in[k, :, at] for k in range(ns - 1)], axis=0)
-        attended[:, at] = (dot(probs[h], vals) / totals[h]).astype(BF16)
-
-    loads[2].wait()
+    attended_all = jnp.concatenate([attended[g] for g in range(groups)], axis=1)
 
     @pl.loop(0, width // tile)
     def _(t):
         at = pl.ds(pl.multiple_of(t * tile, tile), tile)
-        p = dot(attended[...], wo[:, at])
+        p = dot(attended_all, wo[:, at])
         for d in range(nv):
             part[d % 2, d // 2, :, at] = p[d * share : (d + 1) * share]
 
@@ -269,6 +305,9 @@
     share = rows // nv
     nch = nv // 2
     piece = width // ns
+    groups = ns if cols // HD % ns == 0 else 1
+    plane = (groups, rows, cols // groups)
+    landing = (ns - 1, rows, cols // groups)
     dma = pltpu.SemaphoreType.DMA
     vmem = pl.BlockSpec(memory_space=pltpu.VMEM)
     anywhere = pl.BlockSpec(memory_space=pl.ANY)
@@ -285,33 +324,38 @@
             V((count, pixels, width), BF16),
             V((3, width, cols), BF16),
             V((cols, width), BF16),
-            V((count, rows, width), BF16),
+            V((count, nv, share, width), BF16),
+            V((count, nv, share, heads), F32),
             V((2, heads, rows), F32),
             V((nv - 1, 2, heads, rows), F32),
-            V((2, nch, share, width), F32),
-            V((2, nch, share, heads), F32),
+            V((nch, share, width), F32),
+            V((2, nv, share, heads), F32),
             V((nch, share, width), F32),
             V((nch, share, width), F32),
             V((nch - 1, share, width), F32),
             V((share, width), BF16),
             V((nv, share, width), BF16),
-            V((rows, cols), BF16),
-            V((rows, cols), BF16),
-            V((ns - 1, rows, cols), BF16),
-            V((ns - 1, rows, cols), BF16),
-            V((rows, cols), BF16),
-            V((rows, cols), BF16),
+            V(plane, BF16),
+            V(plane, BF16),
+            V(plane, BF16),
+            V(landing, BF16),
+            V(landing, BF16),
+            V(landing, BF16),
+            V(landing, BF16),
+            V(plane, BF16),
             V((2, nch, share, width), F32),
             V((nch, share, width), F32),
             V((nch - 1, share, width), BF16),
             V((nch - 1, share, width), BF16),
             V((ns, share, piece), BF16),
-            dma((3,)),
+            dma((count,)),
+            dma((2,)),
             dma((ns - 1,)), dma((ns - 1,)),
             dma((nv - 1,)), dma((nv - 1,)),
             dma((nch,)), dma((nch,)),
             dma((nch - 1,)), dma((nch - 1,)),
             dma((nch - 1,)), dma((nch - 1,)), dma((nch,)), dma((nch,)),
+            dma((ns - 1,)), dma((ns - 1,)), dma((ns - 1,)), dma((ns - 1,)),
             dma((ns - 1,)), dma((ns - 1,)), dma((ns - 1,)), dma((ns - 1,)),
             dma((nch,)), dma((nch,)),
             dma((nch - 1,)), dma((nch - 1,)),
@@ -326,7 +370,7 @@
         patch_weight,
         var_embed,
         jnp.transpose(agg_query),
-        norm_gain.reshape(1, width),
+        norm_gain,
         jnp.transpose(qkv_weight, (1, 0, 2)),
         out_weight,
         head_cot,

time: 95.1 us -> 90.1 us (0.947)
  Pallas kernels: 90.3 us -> 86.7 us
  local copies, waits for them, and re-layouts: 1.31 us -> 0 us
    pallas_call x1, Pallas kernels: 90.3 us -> 86.7 us  [body(): pl.pallas_call(functools.partial(kernel, nv, ns), out_shape=[jax.ShapeDty...]
    reshape x1 -> x0, local copies, waits for them, and re-layouts: 1.31 us -> none  [body(): norm_gain.reshape(1, width)]
where the time goes in v2:
time: 90.1 us; the launch traced here: 89.9 us
  Pallas kernels  86.7 us (96%)
  matrix products  3.2 us (4%)
    pallas_call x1, Pallas kernels, body(): pl.pallas_call(functools.partial(kernel, nv, ns), out_shape=[jax.ShapeDty...  86.7 us
    dot_general x1, matrix products, body(): lax.dot_general(gathered.reshape(tokens, piece), cot_all.reshape(tokens,...  3.2 us

profile of v2, /device:TPU:0, one launch (start us, length us, event | category | flops | bytes accessed | tf_op | source)
XLA Modules:
  0.0 89.9 jit_solution(16913183949574906084)
XLA Ops:
  0.0 86.7 %shard_map.82 = (bf16[4,8,16,1024]{3,2,1,0:T(8,128)(2,1)}, bf16[4,128,384]{2,1,0:T(8,128)(2,1)}) custom-call(bf16[6,64,128]{2,1,0:T(8,128)(2,1)} %bitcast.11, bf16[6,64,4096]{2,1,0:T(8,128)(2,1)} %pw_hbm.1, bf16[6,4096]{1,0:T(8,128)(2,1)} %var_embed.1, bf16[32,4096]{1,0:T(8,128)(2,1)} %bitcast.10, bf16[4096]{0:T(1024)(128)(2,1)} %gain.1, ...), custom_call_target="tpu_custom_call" | custom-call | tf_op jit(solution)/shard_map/pallas_call | solution.py:315
  86.7 3.2 %fusion = f32[1024,384]{1,0:T(8,128)} fusion(bf16[512,1024]{1,0:T(8,128)(2,1)} %bitcast.8, bf16[512,384]{1,0:T(8,128)(2,1)} %bitcast.9), kind=kOutput, calls=%fused_computation | convolution fusion | flops 402653184 | bytes 3014656 | tf_op jit(solution)/shard_map/dot_general | solution.py:379

commit v3 on v2

--- a/solution.py
+++ b/solution.py
@@ -24,7 +24,7 @@
     patches, pw_hbm, var_embed, query_map, gain, wqkv_hbm, wo_hbm, cot,
     gathered, cot_all,
     pw, wqkv, wo, emb, weights, stats_own, stats_in, for_mate, factor, pair_in, pair_sum, chip_in,
-    agg, normed, keys_own, values_own, query_own, keys_in, values_in, query_in, mixed, attended,
+    agg, normed, keys_own, values_own, query_own, keys_in, values_in, query_in, mixed, attended, products,
     part, pair_in2, pair_sum2, chip_in2, layer,
     pw_sem, local_sem, cot_send, cot_recv, stats_send, stats_recv, pair_send, pair_recv, chip_send, chip_recv,
     norm_send, norm_recv, norm_fsend, norm_frecv, key_send, key_recv, value_send, value_recv,
@@ -39,6 +39,8 @@
     share = rows // nv
     cols = wo.shape[0]
     piece = width // ns
+    half = width // 2
+    sub = piece // 2
     spread_heads = cols // HD % ns == 0
     groups, _, gcols = attended.shape
     me = lax.axis_index("var")
@@ -85,20 +87,20 @@
             for load in loads:
                 load.start()
         pixels = jnp.transpose(patches[v])
-
-        @pl.loop(0, width // tile)
-        def _(t):
-            at = pl.ds(pl.multiple_of(t * tile, tile), tile)
+        s = None
+        for t in range(0, width, tile):
+            at = slice(t, t + tile)
             e = (dot(pixels, pw[v, :, at]) + var_embed[v : v + 1, at].astype(F32)).astype(BF16)
             for d in range(nv):
                 emb[v, d, :, at] = e[d * share : (d + 1) * share]
-
-        scores.append(dot(query_map[...], emb[v].reshape(rows, width), ((1,), (1,))) / math.sqrt(HD))
+            p = dot(e, query_map[:, at], ((1,), (1,)))
+            s = p if s is None else s + p
+        scores.append(s / math.sqrt(HD))
     peak = functools.reduce(jnp.maximum, scores)
     unscaled = [jnp.exp(s - peak) for s in scores]
     total = functools.reduce(jnp.add, unscaled)
-    stats_own[0] = peak
-    stats_own[1] = total
+    stats_own[0] = jnp.transpose(peak)
+    stats_own[1] = jnp.transpose(total)
 
     pl.semaphore_wait(barrier, nv - 1 + ns - 1)
     stats = [
@@ -112,7 +114,7 @@
     cot_all[band] = cot[...]
 
     for v in range(count):
-        w = jnp.transpose(unscaled[v])
+        w = unscaled[v]
         for d in range(nv):
             weights[v, d] = w[d * share : (d + 1) * share]
 
@@ -161,38 +163,60 @@
     for i in range(nch - 1):
         sums = sums + chip_in[i]
     own = sums.astype(BF16)
-    agg[...] = own
+    for a in range(2):
+        for b in range(ns):
+            agg[a, :, b * sub : (b + 1) * sub] = own[:, b * piece + a * sub : b * piece + (a + 1) * sub]
 
     own = own.astype(F32)
     center = jnp.mean(own, axis=-1, keepdims=True)
     shifted = own - center
     spread = jnp.mean(shifted * shifted, axis=-1, keepdims=True)
-    normed[me] = (shifted * lax.rsqrt(spread + eps) * gain[...].astype(F32)[None, :]).astype(BF16)
-
-    def gather(part_of, ssem, rsem, fsend, frecv):
+    own = (shifted * lax.rsqrt(spread + eps) * gain[...].astype(F32)[None, :]).astype(BF16)
+    for a in range(2):
+        normed[a, me] = own[:, a * half : (a + 1) * half]
+
+    def gather_start(part_of, a, ssem, rsem, fsend, frecv):
         mine = part_of(me)
+        at = a * (nch - 1) - 1
         direct = [
-            send(mine, mine, ssem.at[k - 1], rsem.at[k - 1], var=2 * chip_at(k) + core) for k in range(1, nch)
+            send(mine, mine, ssem.at[at + k], rsem.at[at + k], var=2 * chip_at(k) + core) for k in range(1, nch)
         ]
-        across = [send(mine, mine, fsend.at[0], frecv.at[0], var=mate)]
+        return direct, [send(mine, mine, fsend.at[a * nch], frecv.at[a * nch], var=mate)]
+
+    def gather_forward(part_of, a, direct, across, fsend, frecv):
         for k in range(1, nch):
             direct[k - 1].wait_recv()
             got = part_of(2 * chip_from(k) + core)
-            across.append(send(got, got, fsend.at[k], frecv.at[k], var=mate))
+            across.append(send(got, got, fsend.at[a * nch + k], frecv.at[a * nch + k], var=mate))
+
+    def gather_end(across):
         for copy in across:
             copy.wait_recv()
 
-    gather(lambda d: normed.at[d], norm_send, norm_recv, norm_fsend, norm_frecv)
+    norm_parts = [lambda d, a=a: normed.at[a, d] for a in range(2)]
+    started = [
+        gather_start(norm_parts[a], a, norm_send, norm_recv, norm_fsend, norm_frecv) for a in range(2)
+    ]
 
     step = 256
+    gather_forward(norm_parts[0], 0, *started[0], norm_fsend, norm_frecv)
     loads[0].wait()
+    gather_end(started[0][1])
+    for which in (1, 0, 2):
+        for t in range(0, cols, step):
+            at = slice(t, t + step)
+            products[which, :, at] = dot(normed[0].reshape(rows, half), wqkv[which, :half, at])
+    gather_forward(norm_parts[1], 1, *started[1], norm_fsend, norm_frecv)
+    gather_end(started[1][1])
 
     def plane(k):
         return (band + k) % ns if spread_heads else 0
 
     def project(which, out):
         for t in range(cols // step):
-            p = dot(normed[...].reshape(rows, width), wqkv[which, :, t * step : (t + 1) * step]).astype(BF16)
+            tile_at = slice(t * step, (t + 1) * step)
+            p = dot(normed[1].reshape(rows, half), wqkv[which, half:, tile_at])
+            p = (products[which, :, tile_at] + p).astype(BF16)
             span = min(step, gcols)
             for c in range(0, step, span):
                 at = t * step + c
@@ -252,45 +276,53 @@
     loads[1].wait()
     attended_all = jnp.concatenate([attended[g] for g in range(groups)], axis=1)
 
-    @pl.loop(0, width // tile)
-    def _(t):
-        at = pl.ds(pl.multiple_of(t * tile, tile), tile)
-        p = dot(attended_all, wo[:, at])
-        for d in range(nv):
-            part[d % 2, d // 2, :, at] = p[d * share : (d + 1) * share]
-
-    pairs = [
-        send(part.at[1 - core, chip_at(k)], pair_in2.at[i], pair2_send.at[i], pair2_recv.at[i], var=mate)
-        for i, k in enumerate(order)
-    ]
-    chips = []
-    for i, k in enumerate(order):
-        j = chip_at(k)
-        pairs[i].wait_recv()
-        if k:
-            pair_sum2[i] = (part[core, j] + pair_in2[i]).astype(BF16)
-            chips.append(
-                send(pair_sum2.at[i], chip_in2.at[i], chip2_send.at[i], chip2_recv.at[i], var=2 * j + core)
+    pairs = []
+    for a in range(2):
+        for b in range(ns):
+            at = b * piece + a * sub
+            p = dot(attended_all, wo[:, at : at + sub])
+            for d in range(nv):
+                part[a, d % 2, d // 2, :, b * sub : (b + 1) * sub] = p[d * share : (d + 1) * share]
+        pairs.append(send(part.at[a, 1 - core], pair_in2.at[a], pair2_send.at[a], pair2_recv.at[a], var=mate))
+    chips = [[], []]
+    for a in range(2):
+        pairs[a].wait_recv()
+        for k in range(1, nch):
+            j = chip_at(k)
+            pair_sum2[a, k - 1] = (part[a, core, j] + pair_in2[a, j]).astype(BF16)
+            at = a * (nch - 1) + k - 1
+            chips[a].append(
+                send(
+                    pair_sum2.at[a, k - 1], chip_in2.at[a, k - 1], chip2_send.at[at], chip2_recv.at[at],
+                    var=2 * j + core,
+                )
             )
-    sums = agg[...].astype(F32) + (part[core, chip] + pair_in2[nch - 1])
-    for i in range(nch - 1):
-        chips[i].wait_recv()
-        sums = sums + chip_in2[i].astype(F32)
-    sums = sums.astype(BF16)
-    for s in range(ns):
-        layer[s] = sums[:, s * piece : (s + 1) * piece]
-
-    copies = [
-        send(
-            layer.at[(band + k) % ns], gathered.at[band, me], layer_send.at[k - 1], layer_recv.at[k - 1],
-            seq=(band + k) % ns,
-        )
-        for k in range(1, ns)
-    ]
-    gathered[band, me] = layer[band]
-    for copy in copies:
-        copy.wait_recv()
-    gather(lambda d: gathered.at[:, d], last_send, last_recv, last_fsend, last_frecv)
+
+    copies = [[], []]
+    for a in range(2):
+        sums = agg[a].astype(F32) + (part[a, core, chip] + pair_in2[a, chip])
+        for k in range(1, nch):
+            chips[a][k - 1].wait_recv()
+            sums = sums + chip_in2[a, k - 1].astype(F32)
+        sums = sums.astype(BF16)
+        for b in range(ns):
+            layer[a, b] = sums[:, b * sub : (b + 1) * sub]
+        for k in range(1, ns):
+            to, at = (band + k) % ns, a * (ns - 1) + k - 1
+            copies[a].append(
+                send(layer.at[a, to], gathered.at[a, band, me], layer_send.at[at], layer_recv.at[at], seq=to)
+            )
+        gathered[a, band, me] = layer[a, band]
+    last_parts = [lambda d, a=a: gathered.at[a, :, d] for a in range(2)]
+    started = []
+    for a in range(2):
+        for copy in copies[a]:
+            copy.wait_recv()
+        started.append(gather_start(last_parts[a], a, last_send, last_recv, last_fsend, last_frecv))
+    for a in range(2):
+        gather_forward(last_parts[a], a, *started[a], last_fsend, last_frecv)
+    for a in range(2):
+        gather_end(started[a][1])
     for copy in cots:
         copy.wait_recv()
     for copy in pending:
@@ -315,7 +347,7 @@
     gathered, cot_all = pl.pallas_call(
         functools.partial(kernel, nv, ns),
         out_shape=[
-            jax.ShapeDtypeStruct((ns, nv, share, piece), BF16),
+            jax.ShapeDtypeStruct((2, ns, nv, share, piece // 2), BF16),
             jax.ShapeDtypeStruct((ns,) + head_cot.shape, BF16),
         ],
         in_specs=[vmem, anywhere, vmem, vmem, vmem, anywhere, anywhere, vmem],
@@ -333,8 +365,8 @@
             V((nch, share, width), F32),
             V((nch, share, width), F32),
             V((nch - 1, share, width), F32),
-            V((share, width), BF16),
-            V((nv, share, width), BF16),
+            V((2, share, width // 2), BF16),
+            V((2, nv, share, width // 2), BF16),
             V(plane, BF16),
             V(plane, BF16),
             V(plane, BF16),
@@ -343,24 +375,24 @@
             V(landing, BF16),
             V(landing, BF16),
             V(plane, BF16),
-            V((2, nch, share, width), F32),
-            V((nch, share, width), F32),
-            V((nch - 1, share, width), BF16),
-            V((nch - 1, share, width), BF16),
-            V((ns, share, piece), BF16),
-            dma((count,)),
-            dma((2,)),
+            V((3, rows, cols), F32),
+            V((2, 2, nch, share, width // 2), F32),
+            V((2, nch, share, width // 2), F32),
+            V((2, nch - 1, share, width // 2), BF16),
+            V((2, nch - 1, share, width // 2), BF16),
+            V((2, ns, share, piece // 2), BF16),
+            dma((count,)), dma((2,)),
             dma((ns - 1,)), dma((ns - 1,)),
             dma((nv - 1,)), dma((nv - 1,)),
             dma((nch,)), dma((nch,)),
             dma((nch - 1,)), dma((nch - 1,)),
-            dma((nch - 1,)), dma((nch - 1,)), dma((nch,)), dma((nch,)),
+            dma((2 * nch - 2,)), dma((2 * nch - 2,)), dma((2 * nch,)), dma((2 * nch,)),
             dma((ns - 1,)), dma((ns - 1,)), dma((ns - 1,)), dma((ns - 1,)),
             dma((ns - 1,)), dma((ns - 1,)), dma((ns - 1,)), dma((ns - 1,)),
-            dma((nch,)), dma((nch,)),
-            dma((nch - 1,)), dma((nch - 1,)),
-            dma((ns - 1,)), dma((ns - 1,)),
-            dma((nch - 1,)), dma((nch - 1,)), dma((nch,)), dma((nch,)),
+            dma((2,)), dma((2,)),
+            dma((2 * nch - 2,)), dma((2 * nch - 2,)),
+            dma((2 * ns - 2,)), dma((2 * ns - 2,)),
+            dma((2 * nch - 2,)), dma((2 * nch - 2,)), dma((2 * nch,)), dma((2 * nch,)),
         ],
         compiler_params=pltpu.CompilerParams(
             collective_id=0, has_side_effects=True, vmem_limit_bytes=56 * 1024 * 1024
@@ -376,12 +408,13 @@
         head_cot,
     )
     tokens = ns * rows
-    return lax.dot_general(
-        gathered.reshape(tokens, piece),
+    grads = lax.dot_general(
+        gathered.reshape(2, tokens, piece // 2),
         cot_all.reshape(tokens, head_cot.shape[1]),
-        (((0,), (0,)), ((), ())),
+        (((1,), (0,)), ((), ())),
         preferred_element_type=F32,
     )
+    return grads.reshape(piece, head_cot.shape[1])
 
 
 def solution(mesh):

time: 90.1 us -> 80.4 us (0.89)
  Pallas kernels: 86.7 us -> 75.8 us
  local copies, waits for them, and re-layouts: 0 us -> 1.5 us
    pallas_call x1, Pallas kernels: 86.7 us -> 75.8 us  [body(): pl.pallas_call(functools.partial(kernel, nv, ns), out_shape=[jax.ShapeDty...]
    reshape x0 -> x1, local copies, waits for them, and re-layouts: none -> 1.5 us  [body(): gathered.reshape(2, tokens, piece // 2)]
where the time goes in v3:
time: 80.4 us; the launch traced here: 80.1 us
  Pallas kernels  75.8 us (94%)
  matrix products  2.84 us (4%)
  local copies, waits for them, and re-layouts  1.5 us (2%)
    pallas_call x1, Pallas kernels, body(): pl.pallas_call(functools.partial(kernel, nv, ns), out_shape=[jax.ShapeDty...  75.8 us
    dot_general x1, matrix products, body(): lax.dot_general(gathered.reshape(2, tokens, piece // 2), cot_all.reshape(...  2.84 us

profile of v3, /device:TPU:0, one launch (start us, length us, event | category | flops | bytes accessed | tf_op | source)
XLA Modules:
  0.0 80.1 jit_solution(10860437004264914093)
XLA Ops:
  0.0 75.8 %shard_map.82 = (bf16[2,4,8,16,512]{4,3,2,1,0:T(8,128)(2,1)}, bf16[4,128,384]{2,1,0:T(8,128)(2,1)}) custom-call(bf16[6,64,128]{2,1,0:T(8,128)(2,1)} %bitcast.15, bf16[6,64,4096]{2,1,0:T(8,128)(2,1)} %pw_hbm.1, bf16[6,4096]{1,0:T(8,128)(2,1)} %var_embed.1, bf16[32,4096]{1,0:T(8,128)(2,1)} %bitcast.14, bf16[4096]{0:T(1024)(128)(2,1)} %gain.1, ...), custom_call_target="tpu_custom_call" | custom-call | tf_op jit(solution)/shard_map/pallas_call | solution.py:347
  75.8 1.5 %copy.9 = bf16[2,512,512]{1,2,0:T(8,128)(2,1)S(1)} copy(bf16[2,512,512]{2,1,0:T(8,128)(2,1)} %bitcast.12) | data formatting | bytes 2097152 | tf_op jit(solution)/shard_map/reshape | solution.py:412
  77.3 2.8 %fusion = f32[1024,384]{1,0:T(8,128)} fusion(bf16[1024,512]{1,0:T(8,128)(2,1)S(1)} %bitcast.11, bf16[512,384]{1,0:T(8,128)(2,1)} %bitcast.13), kind=kOutput, calls=%fused_computation | convolution fusion | flops 402653184 | bytes 3014656 | tf_op jit(solution)/shard_map/dot_general | solution.py:411

commit v4 on v3

--- a/solution.py
+++ b/solution.py
@@ -1,5 +1,4 @@
 import functools
-import math
 
 import jax
 import jax.numpy as jnp
@@ -48,14 +47,21 @@
     chip = me // 2
     core = me % 2
     mate = chip * 2 + (1 - core)
-    order = list(range(1, nch)) + [0]
+    order = sorted(range(1, nch), key=lambda k: -bin(k).count("1")) + [0]
     pending = []
 
     def chip_at(k):
-        return (chip + k) % nch
-
-    def chip_from(k):
-        return (chip + nch - k) % nch
+        at, place = 0, 1
+        while place < nch:
+            bit = chip // place % 2
+            at = at + place * (1 - bit if k // place % 2 else bit)
+            place *= 2
+        return at
+
+    def settle(upto):
+        for copy in pending[:upto]:
+            copy.wait_send()
+        del pending[:upto]
 
     def send(src, dst, ssem, rsem, **target):
         copy = pltpu.make_async_remote_copy(
@@ -95,7 +101,7 @@
                 emb[v, d, :, at] = e[d * share : (d + 1) * share]
             p = dot(e, query_map[:, at], ((1,), (1,)))
             s = p if s is None else s + p
-        scores.append(s / math.sqrt(HD))
+        scores.append(s * HD**-0.5)
     peak = functools.reduce(jnp.maximum, scores)
     unscaled = [jnp.exp(s - peak) for s in scores]
     total = functools.reduce(jnp.add, unscaled)
@@ -157,6 +163,7 @@
             pair_sum[i, :, at] = acc * own_factor[:, h : h + 1] + pair_in[i, :, at] * mate_factor[:, h : h + 1]
         if k:
             chips.append(send(pair_sum.at[i], chip_in.at[i], chip_send.at[i], chip_recv.at[i], var=d))
+    settle(len(stats) + len(cots) + len(pairs))
     for copy in chips:
         copy.wait_recv()
     sums = pair_sum[nch - 1]
@@ -186,7 +193,7 @@
     def gather_forward(part_of, a, direct, across, fsend, frecv):
         for k in range(1, nch):
             direct[k - 1].wait_recv()
-            got = part_of(2 * chip_from(k) + core)
+            got = part_of(2 * chip_at(k) + core)
             across.append(send(got, got, fsend.at[a * nch + k], frecv.at[a * nch + k], var=mate))
 
     def gather_end(across):
@@ -228,6 +235,7 @@
             for k in range(1, ns)
         ]
 
+    before = len(pending)
     project(1, keys_own)
     copies = to_bands(keys_own, keys_in, key_send, key_recv)
     project(0, query_own)
@@ -235,6 +243,7 @@
         copies += to_bands(query_own, query_in, query_send, query_recv)
     project(2, values_own)
     value_copies = to_bands(values_own, values_in, value_send, value_recv)
+    settle(before)
     for copy in copies:
         copy.wait_recv()
 
@@ -248,7 +257,7 @@
         keys = all_rows(keys_own, keys_in, at)
         for k in sources:
             q = query_in[k - 1, :, at] if k else query_own[plane(0), :, at]
-            s = dot(q, keys, ((1,), (1,))) / math.sqrt(HD)
+            s = dot(q, keys, ((1,), (1,))) * HD**-0.5
             e = jnp.exp(s - jnp.max(s, axis=-1, keepdims=True))
             ready[h, k] = e.astype(BF16), jnp.sum(e, axis=-1, keepdims=True)
     for copy in value_copies:
@@ -276,6 +285,7 @@
     loads[1].wait()
     attended_all = jnp.concatenate([attended[g] for g in range(groups)], axis=1)
 
+    before = len(pending)
     pairs = []
     for a in range(2):
         for b in range(ns):
@@ -310,10 +320,11 @@
         for k in range(1, ns):
             to, at = (band + k) % ns, a * (ns - 1) + k - 1
             copies[a].append(
-                send(layer.at[a, to], gathered.at[a, band, me], layer_send.at[at], layer_recv.at[at], seq=to)
+                send(layer.at[a, to], gathered.at[band, me, :, a * sub : (a + 1) * sub], layer_send.at[at], layer_recv.at[at], seq=to)
             )
-        gathered[a, band, me] = layer[a, band]
-    last_parts = [lambda d, a=a: gathered.at[a, :, d] for a in range(2)]
+        gathered[band, me, :, a * sub : (a + 1) * sub] = layer[a, band]
+    settle(before)
+    last_parts = [lambda d, a=a: gathered.at[:, d, :, a * sub : (a + 1) * sub] for a in range(2)]
     started = []
     for a in range(2):
         for copy in copies[a]:
@@ -321,12 +332,12 @@
         started.append(gather_start(last_parts[a], a, last_send, last_recv, last_fsend, last_frecv))
     for a in range(2):
         gather_forward(last_parts[a], a, *started[a], last_fsend, last_frecv)
+    settle(len(pending) - 2 * (2 * nch - 1))
     for a in range(2):
         gather_end(started[a][1])
     for copy in cots:
         copy.wait_recv()
-    for copy in pending:
-        copy.wait_send()
+    settle(len(pending))
 
 
 def body(nv, ns, patches, patch_weight, var_embed, agg_query, norm_gain, qkv_weight, out_weight, head_cot):
@@ -347,7 +358,7 @@
     gathered, cot_all = pl.pallas_call(
         functools.partial(kernel, nv, ns),
         out_shape=[
-            jax.ShapeDtypeStruct((2, ns, nv, share, piece // 2), BF16),
+            jax.ShapeDtypeStruct((ns, nv, share, piece), BF16),
             jax.ShapeDtypeStruct((ns,) + head_cot.shape, BF16),
         ],
         in_specs=[vmem, anywhere, vmem, vmem, vmem, anywhere, anywhere, vmem],
@@ -408,13 +419,12 @@
         head_cot,
     )
     tokens = ns * rows
-    grads = lax.dot_general(
-        gathered.reshape(2, tokens, piece // 2),
+    return lax.dot_general(
+        gathered.reshape(tokens, piece),
         cot_all.reshape(tokens, head_cot.shape[1]),
-        (((1,), (0,)), ((), ())),
+        (((0,), (0,)), ((), ())),
         preferred_element_type=F32,
     )
-    return grads.reshape(piece, head_cot.shape[1])
 
 
 def solution(mesh):

time: 80.4 us -> 80 us (level)
  local copies, waits for them, and re-layouts: 1.5 us -> 0 us
  Pallas kernels: 75.8 us -> 76.7 us
    reshape x1 -> x0, local copies, waits for them, and re-layouts: 1.5 us -> none  [body(): gathered.reshape(2, tokens, piece // 2)]
    pallas_call x1, Pallas kernels: 75.8 us -> 76.7 us  [body(): pl.pallas_call(functools.partial(kernel, nv, ns), out_shape=[jax.ShapeDty...]
where the time goes in v4:
time: 80 us; the launch traced here: 79.9 us
  Pallas kernels  76.7 us (96%)
  matrix products  3.2 us (4%)
    pallas_call x1, Pallas kernels, body(): pl.pallas_call(functools.partial(kernel, nv, ns), out_shape=[jax.ShapeDty...  76.7 us
    dot_general x1, matrix products, body(): lax.dot_general(gathered.reshape(tokens, piece), cot_all.reshape(tokens,...  3.2 us

profile of v4, /device:TPU:0, one launch (start us, length us, event | category | flops | bytes accessed | tf_op | source)
XLA Modules:
  0.0 79.9 jit_solution(13858069066537073031)
XLA Ops:
  0.0 76.7 %shard_map.82 = (bf16[4,8,16,1024]{3,2,1,0:T(8,128)(2,1)}, bf16[4,128,384]{2,1,0:T(8,128)(2,1)}) custom-call(bf16[6,64,128]{2,1,0:T(8,128)(2,1)} %bitcast.11, bf16[6,64,4096]{2,1,0:T(8,128)(2,1)} %pw_hbm.1, bf16[6,4096]{1,0:T(8,128)(2,1)} %var_embed.1, bf16[32,4096]{1,0:T(8,128)(2,1)} %bitcast.10, bf16[4096]{0:T(1024)(128)(2,1)} %gain.1, ...), custom_call_target="tpu_custom_call" | custom-call | tf_op jit(solution)/shard_map/pallas_call | solution.py:358
  76.7 3.2 %fusion = f32[1024,384]{1,0:T(8,128)} fusion(bf16[512,1024]{1,0:T(8,128)(2,1)} %bitcast.8, bf16[512,384]{1,0:T(8,128)(2,1)} %bitcast.9), kind=kOutput, calls=%fused_computation | convolution fusion | flops 402653184 | bytes 3014656 | tf_op jit(solution)/shard_map/dot_general | solution.py:422

commit v5 on v4

--- a/solution.py
+++ b/solution.py
@@ -155,20 +155,45 @@
             factor[which, d] = scale[d * share : (d + 1) * share]
 
     chips = []
+    cut = slice(0, half), slice(half, width)
     for i, k in enumerate(order):
         d = 2 * chip_at(k) + core
         own_factor, mate_factor = factor[0, d], factor[1, d]
         pairs[i].wait_recv()
         for h, at, acc in weighted(d):
             pair_sum[i, :, at] = acc * own_factor[:, h : h + 1] + pair_in[i, :, at] * mate_factor[:, h : h + 1]
-        if k:
+        if nch != 4 and k:
             chips.append(send(pair_sum.at[i], chip_in.at[i], chip_send.at[i], chip_recv.at[i], var=d))
+        elif k:
+            for a, to in enumerate((1, 2)):
+                if k & to:
+                    slot = 0 if k == 3 else 1
+                    chips.append(
+                        send(
+                            pair_sum.at[i, :, cut[a]], chip_in.at[slot, :, cut[a]],
+                            chip_send.at[len(chips)], chip_recv.at[len(chips)], var=2 * chip_at(to) + core,
+                        )
+                    )
     settle(len(stats) + len(cots) + len(pairs))
-    for copy in chips:
-        copy.wait_recv()
-    sums = pair_sum[nch - 1]
-    for i in range(nch - 1):
-        sums = sums + chip_in[i]
+    if nch == 4:
+        for a, i in enumerate((2, 1)):
+            chips[a].wait_recv()
+            pair_sum[i, :, cut[a]] = pair_sum[i, :, cut[a]] + chip_in[0, :, cut[a]]
+            chips.append(
+                send(
+                    pair_sum.at[i, :, cut[a]], chip_in.at[2, :, cut[a]],
+                    chip_send.at[len(chips)], chip_recv.at[len(chips)], var=2 * chip_at(i) + core,
+                )
+            )
+        for copy in chips[2:]:
+            copy.wait_recv()
+        sums = pair_sum[3] + chip_in[1] + chip_in[2]
+    else:
+        for copy in chips:
+            copy.wait_recv()
+        sums = pair_sum[nch - 1]
+        for i in range(nch - 1):
+            sums = sums + chip_in[i]
     own = sums.astype(BF16)
     for a in range(2):
         for b in range(ns):
@@ -396,7 +421,7 @@
             dma((ns - 1,)), dma((ns - 1,)),
             dma((nv - 1,)), dma((nv - 1,)),
             dma((nch,)), dma((nch,)),
-            dma((nch - 1,)), dma((nch - 1,)),
+            dma((2 * nch - 2,)), dma((2 * nch - 2,)),
             dma((2 * nch - 2,)), dma((2 * nch - 2,)), dma((2 * nch,)), dma((2 * nch,)),
             dma((ns - 1,)), dma((ns - 1,)), dma((ns - 1,)), dma((ns - 1,)),
             dma((ns - 1,)), dma((ns - 1,)), dma((ns - 1,)), dma((ns - 1,)),

time: 80 us -> 76.7 us (0.959)
  Pallas kernels: 76.7 us -> 73.4 us
    pallas_call x1, Pallas kernels: 76.7 us -> 73.4 us  [body(): pl.pallas_call(functools.partial(kernel, nv, ns), out_shape=[jax.ShapeDty...]
where the time goes in v5:
time: 76.7 us; the launch traced here: 76.6 us
  Pallas kernels  73.4 us (96%)
  matrix products  3.2 us (4%)
    pallas_call x1, Pallas kernels, body(): pl.pallas_call(functools.partial(kernel, nv, ns), out_shape=[jax.ShapeDty...  73.4 us
    dot_general x1, matrix products, body(): lax.dot_general(gathered.reshape(tokens, piece), cot_all.reshape(tokens,...  3.2 us

profile of v5, /device:TPU:0, one launch (start us, length us, event | category | flops | bytes accessed | tf_op | source)
XLA Modules:
  0.0 76.6 jit_solution(3981583296002277401)
XLA Ops:
  0.0 73.4 %shard_map.82 = (bf16[4,8,16,1024]{3,2,1,0:T(8,128)(2,1)}, bf16[4,128,384]{2,1,0:T(8,128)(2,1)}) custom-call(bf16[6,64,128]{2,1,0:T(8,128)(2,1)} %bitcast.11, bf16[6,64,4096]{2,1,0:T(8,128)(2,1)} %pw_hbm.1, bf16[6,4096]{1,0:T(8,128)(2,1)} %var_embed.1, bf16[32,4096]{1,0:T(8,128)(2,1)} %bitcast.10, bf16[4096]{0:T(1024)(128)(2,1)} %gain.1, ...), custom_call_target="tpu_custom_call" | custom-call | tf_op jit(solution)/shard_map/pallas_call | solution.py:383
  73.4 3.2 %fusion = f32[1024,384]{1,0:T(8,128)} fusion(bf16[512,1024]{1,0:T(8,128)(2,1)} %bitcast.8, bf16[512,384]{1,0:T(8,128)(2,1)} %bitcast.9), kind=kOutput, calls=%fused_computation | convolution fusion | flops 402653184 | bytes 3014656 | tf_op jit(solution)/shard_map/dot_general | solution.py:447
